TPU v7x, 512 devices: a whole 4x8x8 slice. The times are simulated.
512 devices in a mesh: pipe: 8 (over y), dp: 16 (over x, z_lo), tensor: 4 (over z_hi, core).
Axes of the slice: x: 4, y: 8, z: 8 (z_hi: 2, z_lo: 4; z = z_hi * 4 + z_lo), core: 2. Of those that a mesh axis runs over, the one named last changes fastest.
Arguments:
- handed: bfloat16 [8, 3584, 8192], P('pipe', 'dp', 'tensor'), may hold values from -6 to 6
- cotangent: bfloat16 [8, 3584, 512], P('pipe', 'dp', 'tensor'), may hold values from -6 to 6
- base_weight: bfloat16 [8, 8192, 512], P('pipe', 'tensor'), may hold values from -0.0625 to 0.0625
- adapt_down: bfloat16 [8, 16, 8192, 128], P('pipe', 'dp', 'tensor'), may hold values from -0.0625 to 0.0625
- adapt_up: bfloat16 [8, 16, 128, 512], P('pipe', 'dp', None, 'tensor'), may hold values from -0.5 to 0.5
- row_jobs: int32 [8, 3584, 1], P('pipe', 'dp'), may hold values from 0 to 15; in each aligned block of 224 rows (0 to 223, 224 to 447, ..., all dimensions but the last counted through in order) at most 32 rows name the same one
- job_ranks: int32 [16], replicated, may hold values from 16 to 128
Outputs:
- projected: bfloat16 [8, 3584, 512], P('pipe', 'dp', 'tensor')
- input_grad: bfloat16 [8, 3584, 8192], P('pipe', 'dp', 'tensor')
- down_gradient: bfloat16 [8, 16, 8192, 128], P('pipe', 'dp', 'tensor')
- up_gradient: bfloat16 [8, 16, 128, 512], P('pipe', 'dp', None, 'tensor')
Inputs may be any that keep to these rules, and one draw needn't show every extreme that they name: `row_jobs`: within the rows of one device (aligned blocks of 224 rows) no job appears more than 32 times.
All inputs are finite; a program needn't handle non-finite values.
Results may differ from a plain program's by a relative error of at most 0.0049.
Values may be sent and summed in bfloat16 or wider, within the bound.
A program may use at most 64 MiB of HBM per device.

v0:
```python
import jax
import jax.numpy as jnp
from jax import lax
from jax.sharding import PartitionSpec as P

adapter_alpha = 4.0


def from_behind(x, axis, by):
    size = lax.axis_size(axis)
    return lax.ppermute(x, axis, [(i, (i + by) % size) for i in range(size)])


def inner_sum(left, right):
    return lax.dot_general(
        left, right, (((0,), (0,)), ((), ())), preferred_element_type=jnp.float32
    )


def times_trans(left, right):
    return lax.dot_general(
        left, right, (((1,), (1,)), ((), ())), preferred_element_type=jnp.float32
    )


def shards(handed, cotangent, base_weight, adapt_down, adapt_up, row_jobs, job_ranks):
    inputs = from_behind(handed, "pipe", 1)[0]
    grads_local = cotangent[0]
    grads_full = lax.all_gather(grads_local, "tensor", axis=1, tiled=True)
    weight = base_weight[0]
    base_part = jnp.dot(inputs, weight, preferred_element_type=jnp.float32)
    base_out = lax.psum_scatter(base_part, "tensor", scatter_dimension=1, tiled=True)
    frozen_backward = times_trans(grads_full, weight)
    row_ids = row_jobs[0, :, 0]
    row_count = inputs.shape[0]
    count_of_jobs = lax.axis_size("dp")
    row_capacity = min(row_count, max(32, 2 * row_count // count_of_jobs))
    onehot = (row_ids[:, None] == jnp.arange(count_of_jobs, dtype=jnp.int32)[None, :]).astype(
        jnp.int32
    )
    slot_within = jnp.sum(jnp.cumsum(onehot, 0) * onehot, 1) - 1
    index_of_slot = row_ids * row_capacity + slot_within
    source_rows = (
        jnp.zeros((count_of_jobs * row_capacity,), jnp.int32)
        .at[index_of_slot]
        .set(jnp.arange(row_count, dtype=jnp.int32))
    )
    slot_live = (
        jnp.zeros((count_of_jobs * row_capacity,), jnp.bfloat16)
        .at[index_of_slot]
        .set(jnp.ones((row_count,), jnp.bfloat16))
    )
    send_in = (inputs[source_rows] * slot_live[:, None]).reshape(count_of_jobs, row_capacity, -1)
    send_grad = (grads_local[source_rows] * slot_live[:, None]).reshape(
        count_of_jobs, row_capacity, -1
    )
    recv_in, recv_grad = (
        lax.all_to_all(send_in, "dp", split_axis=0, concat_axis=0, tiled=True),
        lax.all_to_all(send_grad, "dp", split_axis=0, concat_axis=0, tiled=True),
    )
    flat_in = recv_in.reshape(count_of_jobs * row_capacity, -1)
    flat_grad = recv_grad.reshape(count_of_jobs * row_capacity, -1)
    down_local = adapt_down[0, 0]
    local_up_factor = adapt_up[0, 0]
    low_part = jnp.dot(flat_in, down_local, preferred_element_type=jnp.float32)
    grad_part = times_trans(flat_grad, local_up_factor)
    low_sum, grad_sum = lax.psum((low_part, grad_part), "tensor")
    adapter_rank = job_ranks[lax.axis_index("dp")]
    rank_width = down_local.shape[1]
    scale_factor = (
        adapter_alpha
        / jnp.sqrt(adapter_rank.astype(jnp.float32))
        * (jnp.arange(rank_width, dtype=jnp.int32) < adapter_rank).astype(jnp.float32)
    )
    reduced_state = (low_sum * scale_factor).astype(jnp.bfloat16)
    reduced_gradient = (grad_sum * scale_factor).astype(jnp.bfloat16)
    adapter_output = jnp.dot(
        reduced_state, local_up_factor, preferred_element_type=jnp.float32
    ).astype(jnp.bfloat16)
    down_gradient = inner_sum(flat_in, reduced_gradient).astype(jnp.bfloat16)
    up_gradient = inner_sum(reduced_state, flat_grad).astype(jnp.bfloat16)
    slot_back = times_trans(reduced_gradient, down_local).astype(jnp.bfloat16)
    back_out, backward_rows = (
        lax.all_to_all(
            adapter_output.reshape(count_of_jobs, row_capacity, -1),
            "dp",
            split_axis=0,
            concat_axis=0,
            tiled=True,
        ),
        lax.all_to_all(
            slot_back.reshape(count_of_jobs, row_capacity, -1),
            "dp",
            split_axis=0,
            concat_axis=0,
            tiled=True,
        ),
    )
    out_rows = back_out.reshape(count_of_jobs * row_capacity, -1)[index_of_slot]
    adapter_backward = backward_rows.reshape(count_of_jobs * row_capacity, -1)[index_of_slot]
    projected = (base_out + out_rows.astype(jnp.float32)).astype(jnp.bfloat16)
    incoming_gradient = (frozen_backward + adapter_backward.astype(jnp.float32)).astype(
        jnp.bfloat16
    )
    returned = from_behind(incoming_gradient[None], "pipe", -1)
    return (projected[None], returned, down_gradient[None, None], up_gradient[None, None])


def solution(mesh):
    return jax.shard_map(
        shards,
        mesh=mesh,
        in_specs=(
            P("pipe", "dp", "tensor"),
            P("pipe", "dp", "tensor"),
            P("pipe", "tensor", None),
            P("pipe", "dp", "tensor", None),
            P("pipe", "dp", None, "tensor"),
            P("pipe", "dp", None),
            P(),
        ),
        out_specs=(
            P("pipe", "dp", "tensor"),
            P("pipe", "dp", "tensor"),
            P("pipe", "dp", "tensor", None),
            P("pipe", "dp", None, "tensor"),
        ),
        check_vma=False,
    )
```

profile of v0, /device:TPU:1, one launch (start us, length us, event | category | flops | bytes accessed | tf_op | source)
XLA Modules:
  0.0 272.3 jit_solution(15685825030662163780)
XLA Ops:
  7.2 0.0 copy-start
  7.2 4.2 %collective-permute-start = (bf16[1,224,2048]{2,1,0:T(8,128)(2,1)}, bf16[1,224,2048]{2,1,0:T(8,128)(2,1)S(1)}, u32[]{:S(2)}, u32[]{:S(2)}) collective-permute-start(bf16[1,224,2048]{2,1,0:T(8,128)(2,1)} %param.7), channel_id=1, source_target_pairs={{0,64},{64,128},{128,192},{192,256},{256,320},{320,384},{384,448},... | collective-permute-start | bytes 2752520 | tf_op jit(solution)/shard_map/ppermute | solution.py:11
  11.4 0.7 iota_compare_fusion
  12.1 0.6 reduce-window.6
  12.6 0.2 slice_reduce_fusion
  12.9 0.1 bitcast_bitcast_fusion
  12.9 0.7 fusion.15
  13.7 0.7 compare_select_fusion
  14.3 1.3 scatter_custom_fusion
  15.7 2.0 scatter_custom_fusion.1
  17.6 0.1 mul.63
  17.7 1.9 gather_fusion.2
  19.6 0.8 broadcast_multiply_fusion.1
  20.4 9.6 %all-to-all-start.2 = ((bf16[16,32,128]{2,1,0:T(8,128)(2,1)}), bf16[16,32,128]{2,1,0:T(8,128)(2,1)}, u32[]{:S(2)}, u32[]{:S(2)}) async-start(bf16[16,32,128]{2,1,0:T(8,128)(2,1)} %broadcast_multiply_fusion.1), calls=%async_computation.3 | async-start | bytes 262144 | tf_op jit(solution)/shard_map/all_to_all | solution.py:59
  30.0 0.0 collective-permute-done
  30.0 3.3 %gather_fusion = bf16[512,2048]{1,0:T(8,128)(2,1)} fusion(bf16[224,2048]{1,0:T(8,128)(2,1)S(1)} %bitcast.64, s32[1024]{0:T(1024)S(1)} %pad_clamp_fusion.1), kind=kCustom, calls=%fused_computation | custom fusion | bytes 4196352 | tf_op jit(solution)/shard_map/gather | solution.py:53
  33.4 3.1 %broadcast_multiply_fusion = bf16[16,32,2048]{2,1,0:T(8,128)(2,1)} fusion(bf16[16,32,2048]{2,1,0:T(8,128)(2,1)} %bitcast.66, bf16[16,32]{1,0:T(8,128)(2,1)S(1)} %mul.63), kind=kLoop, calls=%fused_computation.18 | loop fusion | flops 1048576 | bytes 4195328 | tf_op jit(solution)/shard_map/mul | solution.py:53
  36.5 0.0 copy-start.2
  36.5 0.9 all-to-all-done.2
  37.3 12.4 %all-to-all-start = ((bf16[16,32,2048]{2,1,0:T(8,128)(2,1)}), bf16[16,32,2048]{2,1,0:T(8,128)(2,1)}, u32[]{:S(2)}, u32[]{:S(2)}) async-start(bf16[16,32,2048]{2,1,0:T(8,128)(2,1)} %broadcast_multiply_fusion), calls=%async_computation.1 | async-start | bytes 4194304 | tf_op jit(solution)/shard_map/all_to_all | solution.py:58
  49.7 0.0 copy-start.6
  49.7 0.0 all-reduce.4.cloned.1.call-start
  49.8 1.8 fusion.12
  51.6 47.9 %all-to-all-done = bf16[16,32,2048]{2,1,0:T(8,128)(2,1)} async-done(((bf16[16,32,2048]{2,1,0:T(8,128)(2,1)}), bf16[16,32,2048]{2,1,0:T(8,128)(2,1)}, u32[]{:S(2)}, u32[]{:S(2)}) %all-to-all-start) | async-done | bytes 2097184 | tf_op jit(solution)/shard_map/all_to_all | solution.py:58
  99.5 0.0 copy-done.2
  99.5 3.0 %fusion.8 = f32[512,128]{1,0:T(8,128)} fusion(bf16[512,2048]{1,0:T(8,128)(2,1)} %bitcast.8, bf16[1,1,2048,128]{3,2,1,0:T(8,128)(2,1)S(1)} %copy-done.2), kind=kOutput, calls=%fused_computation.20 | convolution fusion | flops 268435456 | bytes 2883584 | tf_op jit(solution)/shard_map/dot_general | solution.py:65
  102.5 0.0 all-reduce.4.cloned.1.call-update
  102.5 0.0 copy-done.6
  102.5 0.6 dynamic_slice.3
  103.8 0.6 compare_select_fusion.2
  104.5 63.6 %all-reduce.4.cloned.1.call-done = (f32[512,128]{1,0:T(8,128)}, f32[512,128]{1,0:T(8,128)}) async-done(((f32[512,128]{1,0:T(8,128)}, f32[512,128]{1,0:T(8,128)}), (f32[512,128]{1,0:T(8,128)}, f32[512,128]{1,0:T(8,128)})) %all-reduce.4.cloned.1.call-update) | async-done | bytes 524304 | tf_op jit(solution)/shard_map/psum | solution.py:67
  168.0 3.0 %convolution_convert_fusion = bf16[512,2048]{1,0:T(8,128)(2,1)} fusion(bf16[1,1,2048,128]{3,2,1,0:T(8,128)(2,1)S(1)} %copy-done.2, f32[512,128]{1,0:T(8,128)} %get-tuple-element.5, f32[128]{0:T(128)S(1)} %compare_select_fusion.2), kind=kOutput, calls=%fused_computation.6 | convolution fusion | flops 269615104 | bytes 2884096 | tf_op jit(solution)/shard_map/dot_general | solution.py:21
  171.0 0.0 copy-start.1
  171.0 5.0 %all-to-all-start.3 = ((bf16[16,32,2048]{2,1,0:T(8,128)(2,1)}), bf16[16,32,2048]{2,1,0:T(8,128)(2,1)}, u32[]{:S(2)}, u32[]{:S(2)}) async-start(bf16[16,32,2048]{2,1,0:T(8,128)(2,1)} %bitcast.67), calls=%async_computation.4 | async-start | bytes 4194304 | tf_op jit(solution)/shard_map/all_to_all | solution.py:91
  176.0 0.0 reduce-scatter.2.cloned.1.call-start
  176.0 0.0 copy-done.1
  176.1 41.2 %all-gather = bf16[1,224,512]{2,1,0:T(8,128)(2,1)} all-gather(bf16[1,224,128]{2,1,0:T(8,128)(2,1)S(1)} %copy-done.1), channel_id=2, replica_groups=mesh['pipe'=8,'dp'=16,'tensor'=4] {'tensor'}, dimensions={2}, use_global_device_ids=true | all-gather | bytes 286720 | tf_op jit(solution)/shard_map/all_gather | solution.py:29
  217.2 0.0 copy-done
  217.2 1.4 fusion.4
  218.6 0.0 reduce-scatter.2.cloned.1.call-update
  218.7 9.6 %all-to-all-done.3 = bf16[16,32,2048]{2,1,0:T(8,128)(2,1)} async-done(((bf16[16,32,2048]{2,1,0:T(8,128)(2,1)}), bf16[16,32,2048]{2,1,0:T(8,128)(2,1)}, u32[]{:S(2)}, u32[]{:S(2)}) %all-to-all-start.3) | async-done | bytes 2097184 | tf_op jit(solution)/shard_map/all_to_all | solution.py:91
  228.3 4.0 %gather_fusion.3 = bf16[224,2048]{1,0:T(8,128)(2,1)S(1)} fusion(bf16[512,2048]{1,0:T(8,128)(2,1)} %bitcast.20, s32[1024]{0:T(1024)S(1)} %pad_clamp_fusion), kind=kCustom, calls=%fused_computation.3 | custom fusion | bytes 1835904 | tf_op jit(solution)/shard_map/gather | solution.py:100
  232.3 0.0 copy-start.4
  232.3 0.0 copy-start.5
  232.3 0.0 copy-start.3
  232.3 2.7 fusion.1
  235.0 4.5 %collective-permute-start.1 = (bf16[1,224,2048]{2,1,0:T(8,128)(2,1)}, bf16[1,224,2048]{2,1,0:T(8,128)(2,1)}, u32[]{:S(2)}, u32[]{:S(2)}) collective-permute-start(bf16[1,224,2048]{2,1,0:T(8,128)(2,1)} %fusion.1), channel_id=1, source_target_pairs={{0,448},{64,0},{128,64},{192,128},{256,192},{320,256},{384,320},{4... | collective-permute-start | bytes 2752520 | tf_op jit(solution)/shard_map/ppermute | solution.py:11
  239.5 0.0 copy-done.4
  239.5 0.0 copy-done.5
  239.5 0.8 convolution_convert_fusion.2
  240.3 4.3 %all-to-all-start.1 = ((bf16[16,32,128]{2,1,0:T(8,128)(2,1)}), bf16[16,32,128]{2,1,0:T(8,128)(2,1)S(1)}, u32[]{:S(2)}, u32[]{:S(2)}) async-start(bf16[16,32,128]{2,1,0:T(8,128)(2,1)} %bitcast.12), calls=%async_computation.2 | async-start | bytes 262144 | tf_op jit(solution)/shard_map/all_to_all | solution.py:84
  244.7 1.8 fusion.6
  246.4 0.0 copy-done.3
  246.4 3.1 %fusion.2 = bf16[1,1,2048,128]{3,2,1,0:T(8,128)(2,1)} fusion(bf16[512,2048]{1,0:T(8,128)(2,1)} %bitcast.8, f32[512,128]{1,0:T(8,128)S(1)} %copy-done.3, f32[128]{0:T(128)S(1)} %compare_select_fusion.2), kind=kOutput, calls=%fused_computation.11 | convolution fusion | flops 268828672 | bytes 2884096 | tf_op jit(solution)/shard_map/dot_general | solution.py:15
  249.6 2.3 all-to-all-done.1
  251.9 0.8 gather_fusion.1
  252.7 9.0 %reduce-scatter.2.cloned.1.call-done = f32[224,128]{1,0:T(8,128)} async-done(((f32[224,512]{1,0:T(8,128)}), f32[224,128]{1,0:T(8,128)}) %reduce-scatter.2.cloned.1.call-update) | async-done | bytes 114704 | tf_op jit(solution)/shard_map/reduce_scatter | solution.py:32
  261.7 1.5 fusion.11
  263.3 0.0 collective-permute-done.1
  263.3 2.2 copy.20
  (9 shorter events, 0.1 us)
Async XLA Ops:
  7.2 210.1 %copy-start = (bf16[1,2048,512]{2,1,0:T(8,128)(2,1)S(1)}, bf16[1,2048,512]{2,1,0:T(8,128)(2,1)}, u32[]{:S(2)}) copy-start(bf16[1,2048,512]{2,1,0:T(8,128)(2,1)} %param.9) | copy-start | bytes 6291460
  7.2 22.8 %collective-permute-start = (bf16[1,224,2048]{2,1,0:T(8,128)(2,1)}, bf16[1,224,2048]{2,1,0:T(8,128)(2,1)S(1)}, u32[]{:S(2)}, u32[]{:S(2)}) collective-permute-start(bf16[1,224,2048]{2,1,0:T(8,128)(2,1)} %param.7), channel_id=1, source_target_pairs={{0,64},{64,128},{128,192},{192,256},{256,320},{320,384},{384,448},... | collective-permute-start | bytes 2752520 | tf_op jit(solution)/shard_map/ppermute | solution.py:11
  20.4 16.9 %all-to-all-start.2 = ((bf16[16,32,128]{2,1,0:T(8,128)(2,1)}), bf16[16,32,128]{2,1,0:T(8,128)(2,1)}, u32[]{:S(2)}, u32[]{:S(2)}) async-start(bf16[16,32,128]{2,1,0:T(8,128)(2,1)} %broadcast_multiply_fusion.1), calls=%async_computation.3 | async-start | bytes 262144 | tf_op jit(solution)/shard_map/all_to_all | solution.py:59
  36.5 63.0 %copy-start.2 = (bf16[1,1,2048,128]{3,2,1,0:T(8,128)(2,1)S(1)}, bf16[1,1,2048,128]{3,2,1,0:T(8,128)(2,1)}, u32[]{:S(2)}) copy-start(bf16[1,1,2048,128]{3,2,1,0:T(8,128)(2,1)} %param.10) | copy-start | bytes 1572868
  37.3 62.2 %all-to-all-start = ((bf16[16,32,2048]{2,1,0:T(8,128)(2,1)}), bf16[16,32,2048]{2,1,0:T(8,128)(2,1)}, u32[]{:S(2)}, u32[]{:S(2)}) async-start(bf16[16,32,2048]{2,1,0:T(8,128)(2,1)} %broadcast_multiply_fusion), calls=%async_computation.1 | async-start | bytes 4194304 | tf_op jit(solution)/shard_map/all_to_all | solution.py:58
  49.7 52.8 %copy-start.6 = (s32[16]{0:T(128)S(1)}, s32[16]{0:T(128)}, u32[]{:S(2)}) copy-start(s32[16]{0:T(128)} %param.13) | copy-start | bytes 196
  49.7 118.3 %all-reduce.4.cloned.1.call-start = ((), (), s32[]{:S(2)}) async-start(), calls=%async_computation.6 | async-start | bytes 1048576 | tf_op jit(solution)/shard_map/psum | solution.py:67
  171.0 5.0 %copy-start.1 = (bf16[1,224,128]{2,1,0:T(8,128)(2,1)S(1)}, bf16[1,224,128]{2,1,0:T(8,128)(2,1)}, u32[]{:S(2)}) copy-start(bf16[1,224,128]{2,1,0:T(8,128)(2,1)} %param.8) | copy-start | bytes 172036
  171.0 57.3 %all-to-all-start.3 = ((bf16[16,32,2048]{2,1,0:T(8,128)(2,1)}), bf16[16,32,2048]{2,1,0:T(8,128)(2,1)}, u32[]{:S(2)}, u32[]{:S(2)}) async-start(bf16[16,32,2048]{2,1,0:T(8,128)(2,1)} %bitcast.67), calls=%async_computation.4 | async-start | bytes 4194304 | tf_op jit(solution)/shard_map/all_to_all | solution.py:91
  176.0 85.7 %reduce-scatter.2.cloned.1.call-start = ((), (), s32[]{:S(2)}) async-start(), calls=%async_computation.5 | async-start | bytes 573440 | tf_op jit(solution)/shard_map/reduce_scatter | solution.py:32
  232.3 7.2 %copy-start.4 = (f32[512,128]{1,0:T(8,128)S(1)}, f32[512,128]{1,0:T(8,128)}, u32[]{:S(2)}) copy-start(f32[512,128]{1,0:T(8,128)} %get-tuple-element.4) | copy-start | bytes 786436
  232.3 7.2 %copy-start.5 = (bf16[1,1,128,128]{3,2,1,0:T(8,128)(2,1)S(1)}, bf16[1,1,128,128]{3,2,1,0:T(8,128)(2,1)}, u32[]{:S(2)}) copy-start(bf16[1,1,128,128]{3,2,1,0:T(8,128)(2,1)} %param.11) | copy-start | bytes 98308
  232.3 14.1 %copy-start.3 = (f32[512,128]{1,0:T(8,128)S(1)}, f32[512,128]{1,0:T(8,128)}, u32[]{:S(2)}) copy-start(f32[512,128]{1,0:T(8,128)} %get-tuple-element.5) | copy-start | bytes 786436
  235.0 28.3 %collective-permute-start.1 = (bf16[1,224,2048]{2,1,0:T(8,128)(2,1)}, bf16[1,224,2048]{2,1,0:T(8,128)(2,1)}, u32[]{:S(2)}, u32[]{:S(2)}) collective-permute-start(bf16[1,224,2048]{2,1,0:T(8,128)(2,1)} %fusion.1), channel_id=1, source_target_pairs={{0,448},{64,0},{128,64},{192,128},{256,192},{320,256},{384,320},{4... | collective-permute-start | bytes 2752520 | tf_op jit(solution)/shard_map/ppermute | solution.py:11
  240.3 11.6 %all-to-all-start.1 = ((bf16[16,32,128]{2,1,0:T(8,128)(2,1)}), bf16[16,32,128]{2,1,0:T(8,128)(2,1)S(1)}, u32[]{:S(2)}, u32[]{:S(2)}) async-start(bf16[16,32,128]{2,1,0:T(8,128)(2,1)} %bitcast.12), calls=%async_computation.2 | async-start | bytes 262144 | tf_op jit(solution)/shard_map/all_to_all | solution.py:84
Sparse Core Ops, SparseCore 0:
  102.6 65.3 all-reduce.3
  218.8 42.8 reduce-scatter.1
where the time goes:
time: 273 us; the launch traced here: 272 us
  waiting for transfers between devices  133 us (49%)
  blocking collectives  41.2 us (15%)
  starting transfers between devices  40 us (15%)
  matrix products  17.6 us (6%)
  local copies, waits for them, and re-layouts  16.4 us (6%)
  between operations  14.9 us (5%)
  other arithmetic  8.89 us (3%)
    psum x1, waiting for transfers between devices, shards(): low_sum, grad_sum = lax.psum((low_part, grad_part), 'tensor')  63.6 us
    all_to_all x1, waiting for transfers between devices, shards(): lax.all_to_all(send_in, 'dp', split_axis=0, concat_axis=0, tiled=True)  47.9 us
    all_gather x1, blocking collectives, shards(): grads_full = lax.all_gather(grads_local, 'tensor', axis=1, tiled=True)  41.2 us
    all_to_all x1, starting transfers between devices, shards(): lax.all_to_all(send_in, 'dp', split_axis=0, concat_axis=0, tiled=True)  12.4 us
    all_to_all x1, waiting for transfers between devices, shards(): lax.all_to_all(slot_back.reshape(count_of_jobs, row_capacity, -1), 'dp',...  9.6 us
    all_to_all x1, starting transfers between devices, shards(): lax.all_to_all(send_grad, 'dp', split_axis=0, concat_axis=0, tiled=True)  9.6 us
    reduce_scatter x1, waiting for transfers between devices, shards(): lax.psum_scatter(base_part, 'tensor', scatter_dimension=1, tiled=True)  8.99 us
    ppermute x2, starting transfers between devices, from_behind(): return lax.ppermute(x, axis, [(i, (i + by) % size) for i in range(size)])  8.62 us
  transfers between devices with their start and end apart: 8, of which 6 were waited for; matrix products, arithmetic and copies ran while one was open for 13% of the time, Pallas kernels for 0%

commit v1 on v0

v1 whole, which is shorter than its diff:
```python
import functools

import jax
import jax.numpy as jnp
from jax import lax
from jax.experimental import pallas as pl
from jax.experimental.pallas import tpu as pltpu
from jax.sharding import PartitionSpec as P

ALPHA = 4.0
NX = 4
NZ = 4
CAP = 32
NF = 8
ND = 4
RS0 = 3
XB = 6
YB = 9
LOW = XB + NF - 1
STEPS = LOW + 5
f32, bf16 = jnp.float32, jnp.bfloat16


def nn(a, b):
    return jnp.dot(a, b, preferred_element_type=f32)


def nt(a, b):
    return lax.dot_general(a, b, (((1,), (1,)), ((), ())), preferred_element_type=f32)


def tn(a, b):
    return lax.dot_general(a, b, (((0,), (0,)), ((), ())), preferred_element_type=f32)


def body(
    handed, cot, weight, down, up, jobs, ranks,
    proj, igrad, dgrad, ugrad,
    inp, to_slots, to_rows, xs, xr, cs, cr, cotf, up4, dn4,
    lgp, lgx, lgs, lgz, lg, lgt,
    lwp, lwx, lws, lwz, lw,
    bo, box, bos, boz, base,
    bs, br, los, lor, ybs,
    own, sp, rl, rr, ugs, ugr,
    y_s, y_r, x_s, x_r, c_s, c_r, ct_s, ct_r, up_s, up_r, dn_s, dn_r,
    ex_s, ex_r, b_s, b_r, lo_s, lo_r, yb_s, yb_r, rs_s, rl_r, rr_r, ug_s, ug_r,
):
    rows = inp.shape[1]
    fc = inp.shape[2]
    dc = dn4.shape[1] // ND
    wide = up.shape[3]
    npipe = lax.axis_size("pipe")
    p, d, t = lax.axis_index("pipe"), lax.axis_index("dp"), lax.axis_index("tensor")
    x, z = d // NZ, d % NZ
    c = t % 2
    h = t // 2
    after = {"pipe": (p + 1) % npipe}
    before = {"pipe": (p + npipe - 1) % npipe}
    x_peer = [{"dp": ((x + i) % NX) * NZ + z} for i in range(1, NX)]
    z_peer = [{"dp": x * NZ + (z + i) % NZ} for i in range(1, NZ)]
    z_up = {"dp": x * NZ + jnp.minimum(z + 1, NZ - 1)}
    z_dn = {"dp": x * NZ + jnp.maximum(z - 1, 0)}
    twin = {"tensor": t + 1 - 2 * c}
    far = {"tensor": (t + 2) % 4}

    def remote(src, dst, s, r, who):
        return pltpu.make_async_remote_copy(
            src_ref=src, dst_ref=dst, send_sem=s, recv_sem=r,
            device_id=who, device_id_type=pl.DeviceIdType.MESH,
        )

    bar = pltpu.get_barrier_semaphore()
    everyone = [after, before, twin, far] + x_peer + z_peer
    for who in everyone:
        pl.semaphore_signal(bar, inc=1, device_id=who, device_id_type=pl.DeviceIdType.MESH)

    mine = jobs[0]
    lanes = lax.broadcasted_iota(jnp.int32, (rows, 128), 1)
    hot = (mine == lanes).astype(f32).astype(bf16)
    same = nt(hot, hot)
    i0 = lax.broadcasted_iota(jnp.int32, (rows, rows), 0)
    i1 = lax.broadcasted_iota(jnp.int32, (rows, rows), 1)
    rank_col = jnp.sum(jnp.where(i1 < i0, same, 0.0), axis=1, keepdims=True)
    rank_row = jnp.sum(jnp.where(i0 < i1, same, 0.0), axis=0, keepdims=True)
    slot_col = mine.astype(f32) * CAP + rank_col
    numbers = lax.broadcasted_iota(jnp.int32, (16, 128), 1).astype(f32).astype(bf16)
    slot_row = nt(numbers, hot)[0:1] * CAP + rank_row
    slots = to_slots.shape[0]
    to_rows[...] = (
        lax.broadcasted_iota(jnp.int32, (rows, slots), 1).astype(f32) == slot_col
    ).astype(f32).astype(bf16)
    to_slots[...] = (
        lax.broadcasted_iota(jnp.int32, (slots, rows), 0).astype(f32) == slot_row
    ).astype(f32).astype(bf16)

    def y_copy(f):
        return remote(
            handed.at[0, :, pl.ds(pl.multiple_of(f * fc, fc), fc)], inp.at[f],
            y_s.at[f], y_r.at[f], after,
        )

    def c_copy(i):
        return remote(
            cs.at[(x + i) % NX], cr.at[:, x], c_s.at[i - 1], c_r.at[i - 1], x_peer[i - 1]
        )

    def x_copy(f, i):
        return remote(
            xs.at[f, (x + i) % NX], xr.at[f, :, x], x_s.at[f, i - 1], x_r.at[f, i - 1],
            x_peer[i - 1],
        )

    def b_copy(f, i):
        return remote(
            bs.at[f, :, (x + i) % NX], br.at[f, x], b_s.at[f, i - 1], b_r.at[f, i - 1],
            x_peer[i - 1],
        )

    def lo_copy(i):
        return remote(
            los.at[:, (x + i) % NX], lor.at[x], lo_s.at[i - 1], lo_r.at[i - 1],
            x_peer[i - 1],
        )

    def up_copy(i):
        return remote(up.at[0, 0], up4.at[z], up_s.at[i - 1], up_r.at[i - 1], z_peer[i - 1])

    def ug_copy(i):
        return remote(
            ugs.at[(z + i) % NZ], ugr.at[z], ug_s.at[i - 1], ug_r.at[i - 1], z_peer[i - 1]
        )

    lanes_of = lambda k: cotf.at[:, pl.ds(pl.multiple_of(k * wide, wide), wide)]
    cot_twin = remote(cot.at[0], lanes_of(t), ct_s.at[0], ct_r.at[0], twin)
    cot_far = remote(cot.at[0], lanes_of(t), ct_s.at[1], ct_r.at[1], far)
    cot_on = remote(
        lanes_of((t + 2) % 4), lanes_of((t + 2) % 4), ct_s.at[2], ct_r.at[2], twin
    )

    def dn_part(o, f):
        return dn4.at[o, pl.ds(pl.multiple_of(f * dc, dc), dc)]

    def own_dn(f, way):
        who, k = (z_up, 0) if way > 0 else (z_dn, 1)
        src = down.at[0, 0, pl.ds(pl.multiple_of(f * dc, dc), dc)]
        return remote(src, dn_part(z, f), dn_s.at[z, f, k], dn_r.at[z, f], who)

    def next_dn(o, f, way):
        who, k = (z_up, 0) if way > 0 else (z_dn, 1)
        return remote(dn_part(o, f), dn_part(o, f), dn_s.at[o, f, k], dn_r.at[o, f], who)

    half = lg.shape[0] // 2
    here, there = pl.multiple_of(c * half, half), pl.multiple_of((1 - c) * half, half)
    lg_twin = remote(lgp.at[pl.ds(there, half)], lgx, ex_s.at[0], ex_r.at[0], twin)
    lg_far = remote(lgs, lgz, ex_s.at[1], ex_r.at[1], far)
    lg_swap = remote(
        lg.at[pl.ds(here, half)], lg.at[pl.ds(here, half)], ex_s.at[2], ex_r.at[2], twin
    )
    lw_twin = remote(lwp.at[pl.ds(there, half)], lwx, ex_s.at[3], ex_r.at[3], twin)
    lw_far = remote(lws, lwz, ex_s.at[4], ex_r.at[4], far)
    lw_swap = remote(
        lw.at[pl.ds(here, half)], lw.at[pl.ds(here, half)], ex_s.at[5], ex_r.at[5], twin
    )
    bo_twin = remote(bo.at[1 - c], box, ex_s.at[6], ex_r.at[6], twin)
    bo_far = remote(bos, boz, ex_s.at[7], ex_r.at[7], far)

    def yb_copy(f):
        return remote(
            ybs.at[f], igrad.at[0, :, pl.ds(pl.multiple_of(f * fc, fc), fc)],
            yb_s.at[f], yb_r.at[f], before,
        )

    def rs_up(o, f):
        return remote(sp.at[o, f], rl.at[o, f], rs_s.at[o, f], rl_r.at[o, f], z_up)

    def rs_dn(o, f):
        return remote(sp.at[o, f], rr.at[o, f], rs_s.at[o, f], rr_r.at[o, f], z_dn)

    def each(count, fn):
        def go(i, carry):
            fn(i)
            return carry

        lax.fori_loop(0, count, go, 0)

    pl.semaphore_wait(bar, len(everyone))

    cot_twin.start()
    cot_far.start()
    for i in range(1, NZ):
        up_copy(i).start()
    y_copy(0).start()
    y_copy(1).start()
    for j in range(NX):
        got = nn(to_slots[j * 128 : (j + 1) * 128], cot[0]).astype(bf16)
        cs[j] = got.reshape(NZ, CAP, wide)
    for i in range(1, NX):
        c_copy(i).start()
    for k in range(NZ):
        cr[k, x] = cs[x, k]
    each(NF - 2, lambda f: y_copy(f + 2).start())

    @pl.when(z == 0)
    def _():
        each(ND, lambda f: own_dn(f, 1).start())

    @pl.when(z == NZ - 1)
    def _():
        each(ND, lambda f: own_dn(f, -1).start())

    up4[z] = up[0, 0]
    dn4[z] = down[0, 0]
    cotf[:, pl.ds(pl.multiple_of(t * wide, wide), wide)] = cot[0]
    bo[...] = jnp.zeros_like(bo)
    lwp[...] = jnp.zeros_like(lwp)

    def factor_of(k):
        rank = ranks[x * NZ + k]
        lane = lax.broadcasted_iota(jnp.int32, (1, 128), 1)
        many = jnp.full((1, 128), rank, jnp.int32)
        return jnp.where(lane < many, ALPHA / jnp.sqrt(many.astype(f32)), 0.0)

    def step(s, carry):
        @pl.when(s < NF)
        def _():
            f = s
            y_copy(f).wait_recv()
            block = inp[f]
            for j in range(NX):
                got = nn(to_slots[j * 128 : (j + 1) * 128], block).astype(bf16)
                xs[f, j] = got.reshape(NZ, CAP, fc)
            for i in range(1, NX):
                x_copy(f, i).start()
            for k in range(NZ):
                xr[f, k, x] = xs[f, x, k]
            part = nn(block, weight[0, pl.ds(pl.multiple_of(f * fc, fc), fc)])
            for k in range(4):
                bo[k % 2, k // 2] += part[:, k * wide : (k + 1) * wide]

        @pl.when((s % 3 == 0) & (s < 3 * ND))
        def _():
            @pl.when((z > 0) & (z < NZ - 1))
            def _():
                own_dn(s // 3, 1).start()
                own_dn(s // 3, -1).start()

        for o in range(NZ):
            dist = jnp.abs(z - o)
            g = s - dist
            f = g // 3

            @pl.when((dist > 0) & (g >= 0) & (g % 3 == 0) & (g < 3 * ND))
            def _():
                next_dn(o, f, 1).wait_recv()

                @pl.when((z > o) & (z < NZ - 1))
                def _():
                    next_dn(o, f, 1).start()

                @pl.when((z < o) & (z > 0))
                def _():
                    next_dn(o, f, -1).start()

        @pl.when(s == 0)
        def _():
            cot_far.wait_recv()
            cot_on.start()
            for i in range(1, NX):
                c_copy(i).wait_recv()
            for i in range(1, NZ):
                up_copy(i).wait_recv()
            for k in range(NZ):
                lgp[k * 128 : (k + 1) * 128] = nt(cr[k].reshape(128, wide), up4[k])
            lg_twin.start()

        @pl.when(s == 1)
        def _():
            lg_twin.wait_recv()
            lgx[...] += lgp[pl.ds(here, half)]
            lgs[...] = lgx[...].astype(lgs.dtype)
            lg_far.start()

        @pl.when(s == 2)
        def _():
            lg_far.wait_recv()
            total = lgx[...] + lgz[...].astype(f32)
            for k in range(2):
                lg[pl.ds(pl.multiple_of(c * half + k * 128, 128), 128)] = (
                    total[k * 128 : (k + 1) * 128] * factor_of(2 * c + k)
                ).astype(bf16)
            lg_swap.start()
            cot_twin.wait_recv()
            cot_on.wait_recv()

        @pl.when(s == RS0)
        def _():
            lg_swap.wait_recv()
            for k in range(NZ):
                lgt[k] = lg[k * 128 : (k + 1) * 128].T

        @pl.when((s >= RS0) & (s < RS0 + NF))
        def _():
            f = s - RS0
            for i in range(1, NX):
                x_copy(f, i).wait_recv()
            for k in range(NZ):
                own[k, f] = nn(lgt[k], xr[f, k].reshape(128, fc))

        fu = s - RS0 - z

        @pl.when((fu >= 0) & (fu < NF))
        def _():
            for o in range(1, NZ):

                @pl.when((o > z) & (z == 0))
                def _():
                    sp[o, fu] = own[o, fu].astype(bf16)
                    rs_up(o, fu).start()

                @pl.when((o > z) & (z > 0))
                def _():
                    rs_up(o, fu).wait_recv()
                    sp[o, fu] = (own[o, fu] + rl[o, fu].astype(f32)).astype(bf16)
                    rs_up(o, fu).start()

        fd = s - RS0 - (NZ - 1 - z)

        @pl.when((fd >= 0) & (fd < NF))
        def _():
            for o in range(NZ - 1):

                @pl.when((o < z) & (z == NZ - 1))
                def _():
                    sp[o, fd] = own[o, fd].astype(bf16)
                    rs_dn(o, fd).start()

                @pl.when((o < z) & (z < NZ - 1))
                def _():
                    rs_dn(o, fd).wait_recv()
                    sp[o, fd] = (own[o, fd] + rr[o, fd].astype(f32)).astype(bf16)
                    rs_dn(o, fd).start()

        fe = s - RS0 - (NZ - 1)

        @pl.when((fe >= 0) & (fe < NF))
        def _():
            @pl.when(z > 0)
            def _():
                rs_up(z, fe).wait_recv()
                own[z, fe] += rl[z, fe].astype(f32)

            @pl.when(z < NZ - 1)
            def _():
                rs_dn(z, fe).wait_recv()
                own[z, fe] += rr[z, fe].astype(f32)

            dgrad[0, 0, pl.ds(pl.multiple_of(fe * fc, fc), fc)] = own[z, fe].T.astype(bf16)

        @pl.when((s >= XB) & (s < XB + NF))
        def _():
            f = s - XB
            at = pl.ds(pl.multiple_of(f * fc, fc), fc)
            for k in range(NZ):
                back = nt(lg[k * 128 : (k + 1) * 128], dn4[k, at]).astype(bf16)
                bs[f, k] = back.reshape(NX, CAP, fc)
            for i in range(1, NX):
                b_copy(f, i).start()
            for k in range(NZ):
                br[f, x, k] = bs[f, k, x]
                lwp[k * 128 : (k + 1) * 128] += nn(xr[f, k].reshape(128, fc), dn4[k, at])

        @pl.when(s == NF)
        def _():
            bo_twin.start()

        @pl.when(s == NF + 1)
        def _():
            bo_twin.wait_recv()
            base[...] = bo[c, h] + box[h]
            bos[...] = (bo[c, 1 - h] + box[1 - h]).astype(bos.dtype)
            bo_far.start()

        @pl.when(s == NF + 3)
        def _():
            bo_far.wait_recv()
            base[...] += boz[...].astype(f32)

        @pl.when((s >= YB) & (s < YB + NF))
        def _():
            f = s - YB
            part = nt(cotf[...], weight[0, pl.ds(pl.multiple_of(f * fc, fc), fc)])
            for i in range(1, NX):
                b_copy(f, i).wait_recv()
            ybs[f] = (part + nn(to_rows[...], br[f].reshape(slots, fc))).astype(bf16)
            yb_copy(f).start()

        @pl.when(s == LOW)
        def _():
            lw_twin.start()

        @pl.when(s == LOW + 1)
        def _():
            lw_twin.wait_recv()
            lwx[...] += lwp[pl.ds(here, half)]
            lws[...] = lwx[...].astype(lws.dtype)
            lw_far.start()

        @pl.when(s == LOW + 2)
        def _():
            lw_far.wait_recv()
            total = lwx[...] + lwz[...].astype(f32)
            for k in range(2):
                lw[pl.ds(pl.multiple_of(c * half + k * 128, 128), 128)] = (
                    total[k * 128 : (k + 1) * 128] * factor_of(2 * c + k)
                ).astype(bf16)
            lw_swap.start()

        @pl.when(s == LOW + 3)
        def _():
            lw_swap.wait_recv()
            for k in range(NZ):
                low = lw[k * 128 : (k + 1) * 128]
                los[k] = nn(low, up4[k]).astype(bf16).reshape(NX, CAP, wide)
                ugs[k] = tn(low, cr[k].reshape(128, wide)).astype(bf16)
            for i in range(1, NX):
                lo_copy(i).start()
            for i in range(1, NZ):
                ug_copy(i).start()
            for k in range(NZ):
                lor[x, k] = los[k, x]

        @pl.when(s == LOW + 4)
        def _():
            for i in range(1, NX):
                lo_copy(i).wait_recv()
            proj[0] = (base[...] + nn(to_rows[...], lor[...].reshape(slots, wide))).astype(
                bf16
            )
            ugr[z] = ugs[z]
            for i in range(1, NZ):
                ug_copy(i).wait_recv()
            total = ugr[0].astype(f32)
            for k in range(1, NZ):
                total += ugr[k].astype(f32)
            ugrad[0, 0] = total.astype(bf16)

        return carry

    lax.fori_loop(0, STEPS, step, 0)

    for one in (cot_twin, cot_far, cot_on, lg_twin, lg_far, lg_swap, lw_twin, lw_far,
                lw_swap, bo_twin, bo_far):
        one.wait_send()
    for i in range(1, NX):
        c_copy(i).wait_send()
        lo_copy(i).wait_send()
    for i in range(1, NZ):
        up_copy(i).wait_send()
        ug_copy(i).wait_send()

    def last(f):
        y_copy(f).wait_send()
        for i in range(1, NX):
            x_copy(f, i).wait_send()
            b_copy(f, i).wait_send()
        yb_copy(f).wait_send()
        for o in range(NZ):

            @pl.when(o > z)
            def _():
                rs_up(o, f).wait_send()

            @pl.when(o < z)
            def _():
                rs_dn(o, f).wait_send()

    each(NF, last)

    def last_dn(f):
        for o in range(NZ):

            @pl.when((o <= z) & (z < NZ - 1))
            def _():
                next_dn(o, f, 1).wait_send()

            @pl.when((o >= z) & (z > 0))
            def _():
                next_dn(o, f, -1).wait_send()

    each(ND, last_dn)
    each(NF, lambda f: yb_copy(f).wait_recv())


def shards(handed, cotangent, base_weight, adapt_down, adapt_up, row_jobs, job_ranks):
    _, rows, feats = handed.shape
    wide = cotangent.shape[2]
    out = base_weight.shape[2]
    rank = adapt_down.shape[3]
    fc = feats // NF
    slots = NX * NZ * CAP
    lane = NX * CAP
    half = slots // 2
    v = pltpu.VMEM
    dma = pltpu.SemaphoreType.DMA
    scratch = [
        v((NF, rows, fc), bf16),
        v((slots, rows), bf16),
        v((rows, slots), bf16),
        v((NF, NX, NZ, CAP, fc), bf16),
        v((NF, NZ, NX, CAP, fc), bf16),
        v((NX, NZ, CAP, wide), bf16),
        v((NZ, NX, CAP, wide), bf16),
        v((rows, out), bf16),
        v((NZ, rank, wide), bf16),
        v((NZ, feats, rank), bf16),
        v((slots, rank), f32),
        v((half, rank), f32),
        v((half, rank), bf16),
        v((half, rank), bf16),
        v((slots, rank), bf16),
        v((NZ, rank, lane), bf16),
        v((slots, rank), f32),
        v((half, rank), f32),
        v((half, rank), bf16),
        v((half, rank), bf16),
        v((slots, rank), bf16),
        v((2, 2, rows, wide), f32),
        v((2, rows, wide), f32),
        v((rows, wide), bf16),
        v((rows, wide), bf16),
        v((rows, wide), f32),
        v((NF, NZ, NX, CAP, fc), bf16),
        v((NF, NX, NZ, CAP, fc), bf16),
        v((NZ, NX, CAP, wide), bf16),
        v((NX, NZ, CAP, wide), bf16),
        v((NF, rows, fc), bf16),
        v((NZ, NF, rank, fc), f32),
        v((NZ, NF, rank, fc), bf16),
        v((NZ, NF, rank, fc), bf16),
        v((NZ, NF, rank, fc), bf16),
        v((NZ, rank, wide), bf16),
        v((NZ, rank, wide), bf16),
        dma((NF,)), dma((NF,)),
        dma((NF, NX - 1)), dma((NF, NX - 1)),
        dma((NX - 1,)), dma((NX - 1,)),
        dma((3,)), dma((3,)),
        dma((NZ - 1,)), dma((NZ - 1,)),
        dma((NZ, ND, 2)), dma((NZ, ND)),
        dma((8,)), dma((8,)),
        dma((NF, NX - 1)), dma((NF, NX - 1)),
        dma((NX - 1,)), dma((NX - 1,)),
        dma((NF,)), dma((NF,)),
        dma((NZ, NF)), dma((NZ, NF)), dma((NZ, NF)),
        dma((NZ - 1,)), dma((NZ - 1,)),
    ]
    vm = pl.BlockSpec(memory_space=pltpu.VMEM)
    return pl.pallas_call(
        body,
        out_shape=(
            jax.ShapeDtypeStruct(cotangent.shape, bf16),
            jax.ShapeDtypeStruct(handed.shape, bf16),
            jax.ShapeDtypeStruct(adapt_down.shape, bf16),
            jax.ShapeDtypeStruct(adapt_up.shape, bf16),
        ),
        in_specs=[vm] * 6 + [pl.BlockSpec(memory_space=pltpu.SMEM)],
        out_specs=(vm,) * 4,
        scratch_shapes=scratch,
        compiler_params=pltpu.CompilerParams(
            collective_id=0, has_side_effects=True, vmem_limit_bytes=48 * 2**20
        ),
        name="relay",
    )(handed, cotangent, base_weight, adapt_down, adapt_up, row_jobs, job_ranks)


def solution(mesh):
    return jax.shard_map(
        shards,
        mesh=mesh,
        in_specs=(
            P("pipe", "dp", "tensor"),
            P("pipe", "dp", "tensor"),
            P("pipe", "tensor", None),
            P("pipe", "dp", "tensor", None),
            P("pipe", "dp", None, "tensor"),
            P("pipe", "dp", None),
            P(),
        ),
        out_specs=(
            P("pipe", "dp", "tensor"),
            P("pipe", "dp", "tensor"),
            P("pipe", "dp", "tensor", None),
            P("pipe", "dp", None, "tensor"),
        ),
        check_vma=False,
    )
```

time: 273 us -> 113 us (0.41)
  waiting for transfers between devices: 133 us -> 0 us
  Pallas kernels: 0 us -> 102 us
  blocking collectives: 41.2 us -> 0 us
  starting transfers between devices: 40 us -> 0 us
  matrix products: 17.6 us -> 0 us
  between operations: 14.9 us -> 0.66 us
  other arithmetic: 8.89 us -> 0 us
  local copies, waits for them, and re-layouts: 16.4 us -> 9.79 us
    pallas_call x0 -> x1, Pallas kernels: none -> 102 us  [shards(): pl.pallas_call(body, out_shape=(jax.ShapeDtypeStruct(cotangent.shape, bf1...]
    psum x1 -> x0, waiting for transfers between devices: 63.6 us -> none  [shards(): low_sum, grad_sum = lax.psum((low_part, grad_part), 'tensor')]
    all_to_all x4 -> x0, waiting for transfers between devices: 60.8 us -> none  [the longest x1 47.9 us: shards(): lax.all_to_all(send_in, 'dp', split_axis=0, concat_axis=0, tiled=True)]
    all_gather x1 -> x0, blocking collectives: 41.2 us -> none  [shards(): grads_full = lax.all_gather(grads_local, 'tensor', axis=1, tiled=True)]
    all_to_all x4 -> x0, starting transfers between devices: 31.3 us -> none  [the longest x1 12.4 us: shards(): lax.all_to_all(send_in, 'dp', split_axis=0, concat_axis=0, tiled=True)]
    dot_general x8 -> x0, matrix products: 17.6 us -> none  [the longest x3 7.49 us: times_trans(): lax.dot_general(left, right, (((1,), (1,)), ((), ())), preferred_element_...]
    gather x4 -> x0, local copies, waits for them, and re-layouts: 10 us -> none  [the longest x1 4 us: shards(): backward_rows.reshape(count_of_jobs * row_capacity, -1)[index_of_slot]]
    reduce_scatter x1 -> x0, waiting for transfers between devices: 8.99 us -> none  [shards(): lax.psum_scatter(base_part, 'tensor', scatter_dimension=1, tiled=True)]
  transfers between devices with their start and end apart: 8 -> 0, of which waited for: 6 -> 0; matrix products, arithmetic and copies ran while one was open for 13% -> 0% of each run, Pallas kernels for 0% -> 0%
where the time goes in v1:
time: 113 us; the launch traced here: 112 us
  Pallas kernels  102 us (90%)
  local copies, waits for them, and re-layouts  9.79 us (9%)
    pallas_call x1, Pallas kernels, shards(): pl.pallas_call(body, out_shape=(jax.ShapeDtypeStruct(cotangent.shape, bf1...  102 us
    unnamed x17, local copies, waits for them, and re-layouts  9.79 us

profile of v1, /device:TPU:1, one launch (start us, length us, event | category | flops | bytes accessed | tf_op | source)
XLA Modules:
  0.0 112.4 jit_solution(6394074754058888619)
XLA Ops:
  0.6 0.8 copy.11.jobs
  1.4 0.0 copy-start
  1.4 1.6 %copy-done = bf16[1,2048,512]{2,1,0:T(8,128)(2,1)S(1)} copy-done((bf16[1,2048,512]{2,1,0:T(8,128)(2,1)S(1)}, bf16[1,2048,512]{2,1,0:T(8,128)(2,1)}, u32[]{:S(2)}) %copy-start) | copy-done | bytes 2097176
  3.0 0.0 copy-start.1
  3.0 1.2 %copy-done.1 = bf16[1,224,2048]{2,1,0:T(8,128)(2,1)S(1)} copy-done((bf16[1,224,2048]{2,1,0:T(8,128)(2,1)S(1)}, bf16[1,224,2048]{2,1,0:T(8,128)(2,1)}, u32[]{:S(2)}) %copy-start.1) | copy-done | bytes 917528
  4.2 0.0 copy-start.2
  4.2 1.0 copy-done.2
  5.3 0.0 copy-start.3
  5.3 0.8 copy-done.3
  6.1 0.0 copy-start.4
  6.1 0.8 copy-done.4
  6.8 0.0 copy-start.5
  6.8 0.7 copy-done.5
  7.5 102.0 %relay.1 = (bf16[1,224,128]{2,1,0:T(8,128)(2,1)S(1)}, bf16[1,224,2048]{2,1,0:T(8,128)(2,1)S(1)}, bf16[1,1,2048,128]{3,2,1,0:T(8,128)(2,1)S(1)}, bf16[1,1,128,128]{3,2,1,0:T(8,128)(2,1)S(1)}) custom-call(bf16[1,224,2048]{2,1,0:T(8,128)(2,1)S(1)} %copy-done.1, bf16[1,224,128]{2,1,0:T(8,128)(2,1)S(1)} %copy-done.3, bf16[1,2048,512]{2,1,0:T(8,128)(2,1)S(1)} %copy-done, ...), custom_call_target="tpu_custom_call" | custom-call | tf_op jit(solution)/shard_map/relay/pallas_call | solution.py:557
  109.5 0.6 copy.16
  110.1 0.9 copy.17
  111.0 0.8 copy.18
  111.8 0.6 copy.19
Async XLA Ops:
  1.4 1.6 %copy-start = (bf16[1,2048,512]{2,1,0:T(8,128)(2,1)S(1)}, bf16[1,2048,512]{2,1,0:T(8,128)(2,1)}, u32[]{:S(2)}) copy-start(bf16[1,2048,512]{2,1,0:T(8,128)(2,1)} %weight.1) | copy-start | bytes 6291460
  3.0 1.2 %copy-start.1 = (bf16[1,224,2048]{2,1,0:T(8,128)(2,1)S(1)}, bf16[1,224,2048]{2,1,0:T(8,128)(2,1)}, u32[]{:S(2)}) copy-start(bf16[1,224,2048]{2,1,0:T(8,128)(2,1)} %handed.1) | copy-start | bytes 2752516
  4.2 1.0 copy-start.2
  5.3 0.8 copy-start.3
  6.1 0.8 copy-start.4
  6.8 0.7 copy-start.5

commit v2 on v1

--- a/solution.py
+++ b/solution.py
@@ -13,11 +13,19 @@
 CAP = 32
 NF = 8
 ND = 4
+GP = 2
+GL = 2
 RS0 = 3
+RL = 2
+N0 = 7
 XB = 6
-YB = 9
-LOW = XB + NF - 1
-STEPS = LOW + 5
+YB = 8
+LW0 = 9
+LW = tuple(LW0 + ND - 1 + k for k in (0, 1, 3, 4, 5))
+BO = (NF, NF + 1, NF + 3)
+YL = 8
+STEPS = max(LW[4] + 1, N0 + NF + RL, YB + NF)
+VMEM = 61 * 2**20
 f32, bf16 = jnp.float32, jnp.bfloat16
 
 
@@ -34,8 +42,9 @@
 
 
 def body(
-    handed, cot, weight, down, up, jobs, ranks,
+    handed, cot, weight_in, down, up, jobs_in, ranks_in,
     proj, igrad, dgrad, ugrad,
+    weight, cotv, jobs, ranks, projv, dgv, ugv,
     inp, to_slots, to_rows, xs, xr, cs, cr, cotf, up4, dn4,
     lgp, lgx, lgs, lgz, lg, lgt,
     lwp, lwx, lws, lwz, lw,
@@ -43,7 +52,7 @@
     bs, br, los, lor, ybs,
     own, sp, rl, rr, ugs, ugr,
     y_s, y_r, x_s, x_r, c_s, c_r, ct_s, ct_r, up_s, up_r, dn_s, dn_r,
-    ex_s, ex_r, b_s, b_r, lo_s, lo_r, yb_s, yb_r, rs_s, rl_r, rr_r, ug_s, ug_r,
+    ex_s, ex_r, b_s, b_r, lo_s, lo_r, yb_s, yb_r, rs_s, rl_r, rr_r, ug_s, ug_r, in_s, out_s,
 ):
     rows = inp.shape[1]
     fc = inp.shape[2]
@@ -74,17 +83,29 @@
     for who in everyone:
         pl.semaphore_signal(bar, inc=1, device_id=who, device_id_type=pl.DeviceIdType.MESH)
 
-    mine = jobs[0]
-    lanes = lax.broadcasted_iota(jnp.int32, (rows, 128), 1)
-    hot = (mine == lanes).astype(f32).astype(bf16)
-    same = nt(hot, hot)
+    cot_lanes = pl.ds(pl.multiple_of(t * wide, wide), wide)
+    loads = [
+        pltpu.make_async_copy(src, dst, in_s.at[k])
+        for k, (src, dst) in enumerate([
+            (jobs_in, jobs), (ranks_in, ranks), (cot.at[0], cotv), (up.at[0, 0], up4.at[z]),
+            (down.at[0, 0], dn4.at[z]), (cot.at[0], cotf.at[:, cot_lanes]),
+            (weight_in.at[0], weight),
+        ])
+    ]
+    for one in loads:
+        one.start()
+    loads[0].wait()
+
+    mine = jobs[...]
+    hot = (mine == lax.broadcasted_iota(jnp.int32, (16, rows), 0)).astype(f32).astype(bf16)
+    same = tn(hot, hot)
     i0 = lax.broadcasted_iota(jnp.int32, (rows, rows), 0)
     i1 = lax.broadcasted_iota(jnp.int32, (rows, rows), 1)
     rank_col = jnp.sum(jnp.where(i1 < i0, same, 0.0), axis=1, keepdims=True)
     rank_row = jnp.sum(jnp.where(i0 < i1, same, 0.0), axis=0, keepdims=True)
-    slot_col = mine.astype(f32) * CAP + rank_col
-    numbers = lax.broadcasted_iota(jnp.int32, (16, 128), 1).astype(f32).astype(bf16)
-    slot_row = nt(numbers, hot)[0:1] * CAP + rank_row
+    slot_row = mine.astype(f32) * CAP + rank_row
+    numbers = lax.broadcasted_iota(jnp.int32, (16, 128), 0).astype(f32).astype(bf16)
+    slot_col = tn(hot, numbers)[:, 0:1] * CAP + rank_col
     slots = to_slots.shape[0]
     to_rows[...] = (
         lax.broadcasted_iota(jnp.int32, (rows, slots), 1).astype(f32) == slot_col
@@ -123,7 +144,7 @@
         )
 
     def up_copy(i):
-        return remote(up.at[0, 0], up4.at[z], up_s.at[i - 1], up_r.at[i - 1], z_peer[i - 1])
+        return remote(up4.at[z], up4.at[z], up_s.at[i - 1], up_r.at[i - 1], z_peer[i - 1])
 
     def ug_copy(i):
         return remote(
@@ -139,11 +160,6 @@
 
     def dn_part(o, f):
         return dn4.at[o, pl.ds(pl.multiple_of(f * dc, dc), dc)]
-
-    def own_dn(f, way):
-        who, k = (z_up, 0) if way > 0 else (z_dn, 1)
-        src = down.at[0, 0, pl.ds(pl.multiple_of(f * dc, dc), dc)]
-        return remote(src, dn_part(z, f), dn_s.at[z, f, k], dn_r.at[z, f], who)
 
     def next_dn(o, f, way):
         who, k = (z_up, 0) if way > 0 else (z_dn, 1)
@@ -176,6 +192,13 @@
     def rs_dn(o, f):
         return remote(sp.at[o, f], rr.at[o, f], rs_s.at[o, f], rr_r.at[o, f], z_dn)
 
+    def dg_out(f):
+        at = pl.ds(pl.multiple_of(f * fc, fc), fc)
+        return pltpu.make_async_copy(dgv.at[f], dgrad.at[0, 0, at], out_s.at[f])
+
+    proj_out = pltpu.make_async_copy(projv, proj.at[0], out_s.at[NF])
+    ug_out = pltpu.make_async_copy(ugv, ugrad.at[0, 0], out_s.at[NF + 1])
+
     def each(count, fn):
         def go(i, carry):
             fn(i)
@@ -183,34 +206,35 @@
 
         lax.fori_loop(0, count, go, 0)
 
+    for one in loads[1:5]:
+        one.wait()
+    for j in range(NX):
+        got = nn(to_slots[j * 128 : (j + 1) * 128], cotv[...]).astype(bf16)
+        cs[j] = got.reshape(NZ, CAP, wide)
+
     pl.semaphore_wait(bar, len(everyone))
 
-    cot_twin.start()
-    cot_far.start()
+    for i in range(1, NX):
+        c_copy(i).start()
+    y_copy(0).start()
     for i in range(1, NZ):
         up_copy(i).start()
-    y_copy(0).start()
-    y_copy(1).start()
-    for j in range(NX):
-        got = nn(to_slots[j * 128 : (j + 1) * 128], cot[0]).astype(bf16)
-        cs[j] = got.reshape(NZ, CAP, wide)
-    for i in range(1, NX):
-        c_copy(i).start()
+    cot_far.start()
+    cot_twin.start()
+    each(YL - 1, lambda f: y_copy(f + 1).start())
     for k in range(NZ):
         cr[k, x] = cs[x, k]
-    each(NF - 2, lambda f: y_copy(f + 2).start())
 
     @pl.when(z == 0)
     def _():
-        each(ND, lambda f: own_dn(f, 1).start())
+        each(ND, lambda f: next_dn(0, f, 1).start())
 
     @pl.when(z == NZ - 1)
     def _():
-        each(ND, lambda f: own_dn(f, -1).start())
-
-    up4[z] = up[0, 0]
-    dn4[z] = down[0, 0]
-    cotf[:, pl.ds(pl.multiple_of(t * wide, wide), wide)] = cot[0]
+        each(ND, lambda f: next_dn(NZ - 1, f, -1).start())
+
+    for one in loads[5:]:
+        one.wait()
     bo[...] = jnp.zeros_like(bo)
     lwp[...] = jnp.zeros_like(lwp)
 
@@ -224,6 +248,11 @@
         @pl.when(s < NF)
         def _():
             f = s
+
+            @pl.when(f + YL < NF)
+            def _():
+                y_copy(f + YL).start()
+
             y_copy(f).wait_recv()
             block = inp[f]
             for j in range(NX):
@@ -233,23 +262,23 @@
                 x_copy(f, i).start()
             for k in range(NZ):
                 xr[f, k, x] = xs[f, x, k]
-            part = nn(block, weight[0, pl.ds(pl.multiple_of(f * fc, fc), fc)])
+            part = nn(block, weight[pl.ds(pl.multiple_of(f * fc, fc), fc)])
             for k in range(4):
                 bo[k % 2, k // 2] += part[:, k * wide : (k + 1) * wide]
 
-        @pl.when((s % 3 == 0) & (s < 3 * ND))
+        @pl.when((s % GP == 0) & (s < GP * ND))
         def _():
             @pl.when((z > 0) & (z < NZ - 1))
             def _():
-                own_dn(s // 3, 1).start()
-                own_dn(s // 3, -1).start()
+                next_dn(z, s // GP, 1).start()
+                next_dn(z, s // GP, -1).start()
 
         for o in range(NZ):
             dist = jnp.abs(z - o)
-            g = s - dist
-            f = g // 3
-
-            @pl.when((dist > 0) & (g >= 0) & (g % 3 == 0) & (g < 3 * ND))
+            g = s - GL * dist
+            f = g // GP
+
+            @pl.when((dist > 0) & (g >= 0) & (g % GP == 0) & (g < GP * ND))
             def _():
                 next_dn(o, f, 1).wait_recv()
 
@@ -306,41 +335,55 @@
             for k in range(NZ):
                 own[k, f] = nn(lgt[k], xr[f, k].reshape(128, fc))
 
-        fu = s - RS0 - z
-
-        @pl.when((fu >= 0) & (fu < NF))
-        def _():
-            for o in range(1, NZ):
-
-                @pl.when((o > z) & (z == 0))
-                def _():
-                    sp[o, fu] = own[o, fu].astype(bf16)
-                    rs_up(o, fu).start()
-
-                @pl.when((o > z) & (z > 0))
-                def _():
-                    rs_up(o, fu).wait_recv()
-                    sp[o, fu] = (own[o, fu] + rl[o, fu].astype(f32)).astype(bf16)
-                    rs_up(o, fu).start()
-
-        fd = s - RS0 - (NZ - 1 - z)
-
-        @pl.when((fd >= 0) & (fd < NF))
-        def _():
-            for o in range(NZ - 1):
-
-                @pl.when((o < z) & (z == NZ - 1))
-                def _():
-                    sp[o, fd] = own[o, fd].astype(bf16)
-                    rs_dn(o, fd).start()
-
-                @pl.when((o < z) & (z < NZ - 1))
-                def _():
-                    rs_dn(o, fd).wait_recv()
-                    sp[o, fd] = (own[o, fd] + rr[o, fd].astype(f32)).astype(bf16)
-                    rs_dn(o, fd).start()
-
-        fe = s - RS0 - (NZ - 1)
+        def pass_up(o, f):
+            @pl.when(z == 0)
+            def _():
+                sp[o, f] = own[o, f].astype(bf16)
+
+            @pl.when(z > 0)
+            def _():
+                rs_up(o, f).wait_recv()
+                sp[o, f] = (own[o, f] + rl[o, f].astype(f32)).astype(bf16)
+
+            rs_up(o, f).start()
+
+        def pass_down(o, f):
+            @pl.when(z == NZ - 1)
+            def _():
+                sp[o, f] = own[o, f].astype(bf16)
+
+            @pl.when(z < NZ - 1)
+            def _():
+                rs_dn(o, f).wait_recv()
+                sp[o, f] = (own[o, f] + rr[o, f].astype(f32)).astype(bf16)
+
+            rs_dn(o, f).start()
+
+        fu = s - RS0 - RL * z
+        fd = s - RS0 - RL * (NZ - 1 - z)
+        fn = s - N0
+
+        for o in range(NZ - 1, 1, -1):
+
+            @pl.when((fu >= 0) & (fu < NF) & (o > z + 1))
+            def _():
+                pass_up(o, fu)
+
+        for o in range(NZ - 2):
+
+            @pl.when((fd >= 0) & (fd < NF) & (o < z - 1))
+            def _():
+                pass_down(o, fd)
+
+        @pl.when((fn >= 0) & (fn < NF) & (z < NZ - 1))
+        def _():
+            pass_up(z + 1, fn)
+
+        @pl.when((fn >= 0) & (fn < NF) & (z > 0))
+        def _():
+            pass_down(z - 1, fn)
+
+        fe = s - N0 - RL
 
         @pl.when((fe >= 0) & (fe < NF))
         def _():
@@ -354,7 +397,8 @@
                 rs_dn(z, fe).wait_recv()
                 own[z, fe] += rr[z, fe].astype(f32)
 
-            dgrad[0, 0, pl.ds(pl.multiple_of(fe * fc, fc), fc)] = own[z, fe].T.astype(bf16)
+            dgv[fe] = own[z, fe].T.astype(bf16)
+            dg_out(fe).start()
 
         @pl.when((s >= XB) & (s < XB + NF))
         def _():
@@ -367,20 +411,28 @@
                 b_copy(f, i).start()
             for k in range(NZ):
                 br[f, x, k] = bs[f, k, x]
-                lwp[k * 128 : (k + 1) * 128] += nn(xr[f, k].reshape(128, fc), dn4[k, at])
-
-        @pl.when(s == NF)
+
+        @pl.when((s >= LW0) & (s < LW0 + ND))
+        def _():
+            for i in range(NF // ND):
+                f = (s - LW0) * (NF // ND) + i
+                at = pl.ds(pl.multiple_of(f * fc, fc), fc)
+                for k in range(NZ):
+                    term = nn(xr[f, k].reshape(128, fc), dn4[k, at])
+                    lwp[k * 128 : (k + 1) * 128] += term
+
+        @pl.when(s == BO[0])
         def _():
             bo_twin.start()
 
-        @pl.when(s == NF + 1)
+        @pl.when(s == BO[1])
         def _():
             bo_twin.wait_recv()
             base[...] = bo[c, h] + box[h]
             bos[...] = (bo[c, 1 - h] + box[1 - h]).astype(bos.dtype)
             bo_far.start()
 
-        @pl.when(s == NF + 3)
+        @pl.when(s == BO[2])
         def _():
             bo_far.wait_recv()
             base[...] += boz[...].astype(f32)
@@ -388,24 +440,24 @@
         @pl.when((s >= YB) & (s < YB + NF))
         def _():
             f = s - YB
-            part = nt(cotf[...], weight[0, pl.ds(pl.multiple_of(f * fc, fc), fc)])
+            part = nt(cotf[...], weight[pl.ds(pl.multiple_of(f * fc, fc), fc)])
             for i in range(1, NX):
                 b_copy(f, i).wait_recv()
             ybs[f] = (part + nn(to_rows[...], br[f].reshape(slots, fc))).astype(bf16)
             yb_copy(f).start()
 
-        @pl.when(s == LOW)
+        @pl.when(s == LW[0])
         def _():
             lw_twin.start()
 
-        @pl.when(s == LOW + 1)
+        @pl.when(s == LW[1])
         def _():
             lw_twin.wait_recv()
             lwx[...] += lwp[pl.ds(here, half)]
             lws[...] = lwx[...].astype(lws.dtype)
             lw_far.start()
 
-        @pl.when(s == LOW + 2)
+        @pl.when(s == LW[2])
         def _():
             lw_far.wait_recv()
             total = lwx[...] + lwz[...].astype(f32)
@@ -415,7 +467,7 @@
                 ).astype(bf16)
             lw_swap.start()
 
-        @pl.when(s == LOW + 3)
+        @pl.when(s == LW[3])
         def _():
             lw_swap.wait_recv()
             for k in range(NZ):
@@ -429,20 +481,22 @@
             for k in range(NZ):
                 lor[x, k] = los[k, x]
 
-        @pl.when(s == LOW + 4)
+        @pl.when(s == LW[4])
         def _():
             for i in range(1, NX):
                 lo_copy(i).wait_recv()
-            proj[0] = (base[...] + nn(to_rows[...], lor[...].reshape(slots, wide))).astype(
+            projv[...] = (base[...] + nn(to_rows[...], lor[...].reshape(slots, wide))).astype(
                 bf16
             )
+            proj_out.start()
             ugr[z] = ugs[z]
             for i in range(1, NZ):
                 ug_copy(i).wait_recv()
             total = ugr[0].astype(f32)
             for k in range(1, NZ):
                 total += ugr[k].astype(f32)
-            ugrad[0, 0] = total.astype(bf16)
+            ugv[...] = total.astype(bf16)
+            ug_out.start()
 
         return carry
 
@@ -488,7 +542,29 @@
                 next_dn(o, f, -1).wait_send()
 
     each(ND, last_dn)
+    each(NF, lambda f: dg_out(f).wait())
+    proj_out.wait()
+    ug_out.wait()
     each(NF, lambda f: yb_copy(f).wait_recv())
+
+
+def flush(*refs):
+    ins, outs, mids, sems = refs[:4], refs[4:8], refs[8:12], refs[12]
+    first = [
+        pltpu.make_async_copy(src, mid, sems.at[0, k])
+        for k, (src, mid) in enumerate(zip(ins, mids))
+    ]
+    second = [
+        pltpu.make_async_copy(mid, dst, sems.at[1, k])
+        for k, (mid, dst) in enumerate(zip(mids, outs))
+    ]
+    for k in (1, 2, 0, 3):
+        first[k].start()
+    for k in (1, 2, 0, 3):
+        first[k].wait()
+        second[k].start()
+    for one in second:
+        one.wait()
 
 
 def shards(handed, cotangent, base_weight, adapt_down, adapt_up, row_jobs, job_ranks):
@@ -503,6 +579,13 @@
     v = pltpu.VMEM
     dma = pltpu.SemaphoreType.DMA
     scratch = [
+        v((feats, out), bf16),
+        v((rows, wide), bf16),
+        v((1, rows), jnp.int32),
+        pltpu.SMEM(job_ranks.shape, jnp.int32),
+        v((rows, wide), bf16),
+        v((NF, fc, rank), bf16),
+        v((rank, wide), bf16),
         v((NF, rows, fc), bf16),
         v((slots, rows), bf16),
         v((rows, slots), bf16),
@@ -552,24 +635,36 @@
         dma((NF,)), dma((NF,)),
         dma((NZ, NF)), dma((NZ, NF)), dma((NZ, NF)),
         dma((NZ - 1,)), dma((NZ - 1,)),
+        dma((7,)),
+        dma((NF + 2,)),
     ]
-    vm = pl.BlockSpec(memory_space=pltpu.VMEM)
-    return pl.pallas_call(
+    hbm = pl.BlockSpec(memory_space=pltpu.HBM)
+    shapes = (
+        jax.ShapeDtypeStruct(cotangent.shape, bf16),
+        jax.ShapeDtypeStruct(handed.shape, bf16),
+        jax.ShapeDtypeStruct(adapt_down.shape, bf16),
+        jax.ShapeDtypeStruct(adapt_up.shape, bf16),
+    )
+    results = pl.pallas_call(
         body,
-        out_shape=(
-            jax.ShapeDtypeStruct(cotangent.shape, bf16),
-            jax.ShapeDtypeStruct(handed.shape, bf16),
-            jax.ShapeDtypeStruct(adapt_down.shape, bf16),
-            jax.ShapeDtypeStruct(adapt_up.shape, bf16),
-        ),
-        in_specs=[vm] * 6 + [pl.BlockSpec(memory_space=pltpu.SMEM)],
-        out_specs=(vm,) * 4,
+        out_shape=shapes,
+        in_specs=[hbm] * 7,
+        out_specs=(hbm,) * 4,
         scratch_shapes=scratch,
         compiler_params=pltpu.CompilerParams(
-            collective_id=0, has_side_effects=True, vmem_limit_bytes=48 * 2**20
+            collective_id=0, has_side_effects=True, vmem_limit_bytes=VMEM
         ),
         name="relay",
-    )(handed, cotangent, base_weight, adapt_down, adapt_up, row_jobs, job_ranks)
+    )(handed, cotangent, base_weight, adapt_down, adapt_up, row_jobs.reshape(1, rows), job_ranks)
+    return pl.pallas_call(
+        flush,
+        out_shape=shapes,
+        in_specs=[hbm] * 4,
+        out_specs=(hbm,) * 4,
+        scratch_shapes=[v(one.shape, one.dtype) for one in shapes] + [dma((2, 4))],
+        compiler_params=pltpu.CompilerParams(vmem_limit_bytes=VMEM),
+        name="flush",
+    )(*results)
 
 
 def solution(mesh):

time: 113 us -> 90.4 us (0.80)
  Pallas kernels: 102 us -> 89.6 us
  local copies, waits for them, and re-layouts: 9.79 us -> 0 us
    pallas_call x1 -> x2, Pallas kernels: 102 us -> 89.6 us  [the longest x1 87.2 us: shards(): pl.pallas_call(body, out_shape=shapes, in_specs=[hbm] * 7, out_specs=(hbm...]
    unnamed x17 -> x0, local copies, waits for them, and re-layouts: 9.79 us -> none
where the time goes in v2:
time: 90.4 us; the launch traced here: 90.2 us
  Pallas kernels  89.6 us (99%)
    pallas_call x1, Pallas kernels, shards(): pl.pallas_call(body, out_shape=shapes, in_specs=[hbm] * 7, out_specs=(hbm...  87.2 us
    pallas_call x1, Pallas kernels, shards(): pl.pallas_call(flush, out_shape=shapes, in_specs=[hbm] * 4, out_specs=(hb...  2.36 us

profile of v2, /device:TPU:1, one launch (start us, length us, event | category | flops | bytes accessed | tf_op | source)
XLA Modules:
  0.0 90.2 jit_solution(6587629610955941097)
XLA Ops:
  0.6 87.2 %relay.1 = (bf16[1,224,128]{2,1,0:T(8,128)(2,1)}, bf16[1,224,2048]{2,1,0:T(8,128)(2,1)}, bf16[1,1,2048,128]{3,2,1,0:T(8,128)(2,1)}, bf16[1,1,128,128]{3,2,1,0:T(8,128)(2,1)}) custom-call(bf16[1,224,2048]{2,1,0:T(8,128)(2,1)} %handed.1, bf16[1,224,128]{2,1,0:T(8,128)(2,1)} %cot.1, bf16[1,2048,512]{2,1,0:T(8,128)(2,1)} %weight_in.1, ...), custom_call_target="tpu_custom_call" | custom-call | tf_op jit(solution)/shard_map/relay/pallas_call | solution.py:648
  87.9 2.4 %flush.1 = (bf16[1,224,128]{2,1,0:T(8,128)(2,1)}, bf16[1,224,2048]{2,1,0:T(8,128)(2,1)}, bf16[1,1,2048,128]{3,2,1,0:T(8,128)(2,1)}, bf16[1,1,128,128]{3,2,1,0:T(8,128)(2,1)}) custom-call(bf16[1,224,128]{2,1,0:T(8,128)(2,1)} %get-tuple-element.8.refs_0_, bf16[1,224,2048]{2,1,0:T(8,128)(2,1)} %get-tuple-element.9.refs_1_, ...), custom_call_target="tpu_custom_call" | custom-call | tf_op jit(solution)/shard_map/flush/pallas_call | solution.py:659

commit v3 on v2

--- a/solution.py
+++ b/solution.py
@@ -22,9 +22,10 @@
 YB = 8
 LW0 = 9
 LW = tuple(LW0 + ND - 1 + k for k in (0, 1, 3, 4, 5))
-BO = (NF, NF + 1, NF + 3)
+BO = (11, 12, 14)
 YL = 8
-STEPS = max(LW[4] + 1, N0 + NF + RL, YB + NF)
+END = max(N0, YB) + 2
+STEPS = max(LW[4] + 1, N0 + NF + RL, END + NF)
 VMEM = 61 * 2**20
 f32, bf16 = jnp.float32, jnp.bfloat16
 
@@ -94,25 +95,7 @@
     ]
     for one in loads:
         one.start()
-    loads[0].wait()
-
-    mine = jobs[...]
-    hot = (mine == lax.broadcasted_iota(jnp.int32, (16, rows), 0)).astype(f32).astype(bf16)
-    same = tn(hot, hot)
-    i0 = lax.broadcasted_iota(jnp.int32, (rows, rows), 0)
-    i1 = lax.broadcasted_iota(jnp.int32, (rows, rows), 1)
-    rank_col = jnp.sum(jnp.where(i1 < i0, same, 0.0), axis=1, keepdims=True)
-    rank_row = jnp.sum(jnp.where(i0 < i1, same, 0.0), axis=0, keepdims=True)
-    slot_row = mine.astype(f32) * CAP + rank_row
-    numbers = lax.broadcasted_iota(jnp.int32, (16, 128), 0).astype(f32).astype(bf16)
-    slot_col = tn(hot, numbers)[:, 0:1] * CAP + rank_col
     slots = to_slots.shape[0]
-    to_rows[...] = (
-        lax.broadcasted_iota(jnp.int32, (rows, slots), 1).astype(f32) == slot_col
-    ).astype(f32).astype(bf16)
-    to_slots[...] = (
-        lax.broadcasted_iota(jnp.int32, (slots, rows), 0).astype(f32) == slot_row
-    ).astype(f32).astype(bf16)
 
     def y_copy(f):
         return remote(
@@ -122,24 +105,24 @@
 
     def c_copy(i):
         return remote(
-            cs.at[(x + i) % NX], cr.at[:, x], c_s.at[i - 1], c_r.at[i - 1], x_peer[i - 1]
+            cs.at[(x + i) % NX], cr.at[x], c_s.at[i - 1], c_r.at[i - 1], x_peer[i - 1]
         )
 
     def x_copy(f, i):
         return remote(
-            xs.at[f, (x + i) % NX], xr.at[f, :, x], x_s.at[f, i - 1], x_r.at[f, i - 1],
+            xs.at[f, (x + i) % NX], xr.at[f, x], x_s.at[f, i - 1], x_r.at[f, i - 1],
             x_peer[i - 1],
         )
 
     def b_copy(f, i):
         return remote(
-            bs.at[f, :, (x + i) % NX], br.at[f, x], b_s.at[f, i - 1], b_r.at[f, i - 1],
+            bs.at[f, (x + i) % NX], br.at[f, x], b_s.at[f, i - 1], b_r.at[f, i - 1],
             x_peer[i - 1],
         )
 
     def lo_copy(i):
         return remote(
-            los.at[:, (x + i) % NX], lor.at[x], lo_s.at[i - 1], lo_r.at[i - 1],
+            los.at[(x + i) % NX], lor.at[x], lo_s.at[i - 1], lo_r.at[i - 1],
             x_peer[i - 1],
         )
 
@@ -206,32 +189,49 @@
 
         lax.fori_loop(0, count, go, 0)
 
+    pl.semaphore_wait(bar, len(everyone))
+
+    y_copy(0).start()
+    cot_far.start()
+    cot_twin.start()
+    each(YL - 1, lambda f: y_copy(f + 1).start())
     for one in loads[1:5]:
         one.wait()
+    for i in range(1, NZ):
+        up_copy(i).start()
+
+    @pl.when(z == 0)
+    def _():
+        each(ND, lambda f: next_dn(0, f, 1).start())
+
+    @pl.when(z == NZ - 1)
+    def _():
+        each(ND, lambda f: next_dn(NZ - 1, f, -1).start())
+
+    loads[0].wait()
+
+    mine = jobs[...]
+    hot = (mine == lax.broadcasted_iota(jnp.int32, (16, rows), 0)).astype(f32).astype(bf16)
+    same = tn(hot, hot)
+    i0 = lax.broadcasted_iota(jnp.int32, (rows, rows), 0)
+    i1 = lax.broadcasted_iota(jnp.int32, (rows, rows), 1)
+    rank_col = jnp.sum(jnp.where(i1 < i0, same, 0.0), axis=1, keepdims=True)
+    rank_row = jnp.sum(jnp.where(i0 < i1, same, 0.0), axis=0, keepdims=True)
+    slot_row = mine.astype(f32) * CAP + rank_row
+    numbers = lax.broadcasted_iota(jnp.int32, (16, 128), 0).astype(f32).astype(bf16)
+    slot_col = tn(hot, numbers)[:, 0:1] * CAP + rank_col
+    to_rows[...] = (
+        lax.broadcasted_iota(jnp.int32, (rows, slots), 1).astype(f32) == slot_col
+    ).astype(f32).astype(bf16)
+    to_slots[...] = (
+        lax.broadcasted_iota(jnp.int32, (slots, rows), 0).astype(f32) == slot_row
+    ).astype(f32).astype(bf16)
     for j in range(NX):
         got = nn(to_slots[j * 128 : (j + 1) * 128], cotv[...]).astype(bf16)
         cs[j] = got.reshape(NZ, CAP, wide)
-
-    pl.semaphore_wait(bar, len(everyone))
-
     for i in range(1, NX):
         c_copy(i).start()
-    y_copy(0).start()
-    for i in range(1, NZ):
-        up_copy(i).start()
-    cot_far.start()
-    cot_twin.start()
-    each(YL - 1, lambda f: y_copy(f + 1).start())
-    for k in range(NZ):
-        cr[k, x] = cs[x, k]
-
-    @pl.when(z == 0)
-    def _():
-        each(ND, lambda f: next_dn(0, f, 1).start())
-
-    @pl.when(z == NZ - 1)
-    def _():
-        each(ND, lambda f: next_dn(NZ - 1, f, -1).start())
+    cr[x] = cs[x]
 
     for one in loads[5:]:
         one.wait()
@@ -243,6 +243,22 @@
         lane = lax.broadcasted_iota(jnp.int32, (1, 128), 1)
         many = jnp.full((1, 128), rank, jnp.int32)
         return jnp.where(lane < many, ALPHA / jnp.sqrt(many.astype(f32)), 0.0)
+
+    def last(f):
+        y_copy(f).wait_send()
+        for i in range(1, NX):
+            x_copy(f, i).wait_send()
+            b_copy(f, i).wait_send()
+        yb_copy(f).wait_send()
+        for o in range(NZ):
+
+            @pl.when(o > z)
+            def _():
+                rs_up(o, f).wait_send()
+
+            @pl.when(o < z)
+            def _():
+                rs_dn(o, f).wait_send()
 
     def step(s, carry):
         @pl.when(s < NF)
@@ -260,8 +276,7 @@
                 xs[f, j] = got.reshape(NZ, CAP, fc)
             for i in range(1, NX):
                 x_copy(f, i).start()
-            for k in range(NZ):
-                xr[f, k, x] = xs[f, x, k]
+            xr[f, x] = xs[f, x]
             part = nn(block, weight[pl.ds(pl.multiple_of(f * fc, fc), fc)])
             for k in range(4):
                 bo[k % 2, k // 2] += part[:, k * wide : (k + 1) * wide]
@@ -299,7 +314,7 @@
             for i in range(1, NZ):
                 up_copy(i).wait_recv()
             for k in range(NZ):
-                lgp[k * 128 : (k + 1) * 128] = nt(cr[k].reshape(128, wide), up4[k])
+                lgp[k * 128 : (k + 1) * 128] = nt(cr[:, k].reshape(128, wide), up4[k])
             lg_twin.start()
 
         @pl.when(s == 1)
@@ -333,7 +348,7 @@
             for i in range(1, NX):
                 x_copy(f, i).wait_recv()
             for k in range(NZ):
-                own[k, f] = nn(lgt[k], xr[f, k].reshape(128, fc))
+                own[k, f] = nn(lgt[k], xr[f, :, k].reshape(128, fc))
 
         def pass_up(o, f):
             @pl.when(z == 0)
@@ -406,11 +421,10 @@
             at = pl.ds(pl.multiple_of(f * fc, fc), fc)
             for k in range(NZ):
                 back = nt(lg[k * 128 : (k + 1) * 128], dn4[k, at]).astype(bf16)
-                bs[f, k] = back.reshape(NX, CAP, fc)
+                bs[f, :, k] = back.reshape(NX, CAP, fc)
             for i in range(1, NX):
                 b_copy(f, i).start()
-            for k in range(NZ):
-                br[f, x, k] = bs[f, k, x]
+            br[f, x] = bs[f, x]
 
         @pl.when((s >= LW0) & (s < LW0 + ND))
         def _():
@@ -418,7 +432,7 @@
                 f = (s - LW0) * (NF // ND) + i
                 at = pl.ds(pl.multiple_of(f * fc, fc), fc)
                 for k in range(NZ):
-                    term = nn(xr[f, k].reshape(128, fc), dn4[k, at])
+                    term = nn(xr[f, :, k].reshape(128, fc), dn4[k, at])
                     lwp[k * 128 : (k + 1) * 128] += term
 
         @pl.when(s == BO[0])
@@ -472,14 +486,13 @@
             lw_swap.wait_recv()
             for k in range(NZ):
                 low = lw[k * 128 : (k + 1) * 128]
-                los[k] = nn(low, up4[k]).astype(bf16).reshape(NX, CAP, wide)
-                ugs[k] = tn(low, cr[k].reshape(128, wide)).astype(bf16)
+                los[:, k] = nn(low, up4[k]).astype(bf16).reshape(NX, CAP, wide)
+                ugs[k] = tn(low, cr[:, k].reshape(128, wide)).astype(bf16)
             for i in range(1, NX):
                 lo_copy(i).start()
             for i in range(1, NZ):
                 ug_copy(i).start()
-            for k in range(NZ):
-                lor[x, k] = los[k, x]
+            lor[x] = los[x]
 
         @pl.when(s == LW[4])
         def _():
@@ -498,6 +511,10 @@
             ugv[...] = total.astype(bf16)
             ug_out.start()
 
+        @pl.when((s >= END) & (s < END + NF))
+        def _():
+            last(s - END)
+
         return carry
 
     lax.fori_loop(0, STEPS, step, 0)
@@ -512,23 +529,6 @@
         up_copy(i).wait_send()
         ug_copy(i).wait_send()
 
-    def last(f):
-        y_copy(f).wait_send()
-        for i in range(1, NX):
-            x_copy(f, i).wait_send()
-            b_copy(f, i).wait_send()
-        yb_copy(f).wait_send()
-        for o in range(NZ):
-
-            @pl.when(o > z)
-            def _():
-                rs_up(o, f).wait_send()
-
-            @pl.when(o < z)
-            def _():
-                rs_dn(o, f).wait_send()
-
-    each(NF, last)
 
     def last_dn(f):
         for o in range(NZ):
@@ -590,9 +590,9 @@
         v((slots, rows), bf16),
         v((rows, slots), bf16),
         v((NF, NX, NZ, CAP, fc), bf16),
-        v((NF, NZ, NX, CAP, fc), bf16),
+        v((NF, NX, NZ, CAP, fc), bf16),
         v((NX, NZ, CAP, wide), bf16),
-        v((NZ, NX, CAP, wide), bf16),
+        v((NX, NZ, CAP, wide), bf16),
         v((rows, out), bf16),
         v((NZ, rank, wide), bf16),
         v((NZ, feats, rank), bf16),
@@ -612,9 +612,9 @@
         v((rows, wide), bf16),
         v((rows, wide), bf16),
         v((rows, wide), f32),
-        v((NF, NZ, NX, CAP, fc), bf16),
         v((NF, NX, NZ, CAP, fc), bf16),
-        v((NZ, NX, CAP, wide), bf16),
+        v((NF, NX, NZ, CAP, fc), bf16),
+        v((NX, NZ, CAP, wide), bf16),
         v((NX, NZ, CAP, wide), bf16),
         v((NF, rows, fc), bf16),
         v((NZ, NF, rank, fc), f32),

time: 90.4 us -> 89.8 us (level)
  no operation moved by 1% of the time
where the time goes in v3:
time: 89.8 us; the launch traced here: 89.7 us
  Pallas kernels  89 us (99%)
    pallas_call x1, Pallas kernels, shards(): pl.pallas_call(body, out_shape=shapes, in_specs=[hbm] * 7, out_specs=(hbm...  86.7 us
    pallas_call x1, Pallas kernels, shards(): pl.pallas_call(flush, out_shape=shapes, in_specs=[hbm] * 4, out_specs=(hb...  2.36 us

profile of v3, /device:TPU:1, one launch (start us, length us, event | category | flops | bytes accessed | tf_op | source)
XLA Modules:
  0.0 89.7 jit_solution(9474552637763553301)
XLA Ops:
  0.6 86.7 %relay.1 = (bf16[1,224,128]{2,1,0:T(8,128)(2,1)}, bf16[1,224,2048]{2,1,0:T(8,128)(2,1)}, bf16[1,1,2048,128]{3,2,1,0:T(8,128)(2,1)}, bf16[1,1,128,128]{3,2,1,0:T(8,128)(2,1)}) custom-call(bf16[1,224,2048]{2,1,0:T(8,128)(2,1)} %handed.1, bf16[1,224,128]{2,1,0:T(8,128)(2,1)} %cot.1, bf16[1,2048,512]{2,1,0:T(8,128)(2,1)} %weight_in.1, ...), custom_call_target="tpu_custom_call" | custom-call | tf_op jit(solution)/shard_map/relay/pallas_call | solution.py:648
  87.3 2.4 %flush.1 = (bf16[1,224,128]{2,1,0:T(8,128)(2,1)}, bf16[1,224,2048]{2,1,0:T(8,128)(2,1)}, bf16[1,1,2048,128]{3,2,1,0:T(8,128)(2,1)}, bf16[1,1,128,128]{3,2,1,0:T(8,128)(2,1)}) custom-call(bf16[1,224,128]{2,1,0:T(8,128)(2,1)} %get-tuple-element.8.refs_0_, bf16[1,224,2048]{2,1,0:T(8,128)(2,1)} %get-tuple-element.9.refs_1_, ...), custom_call_target="tpu_custom_call" | custom-call | tf_op jit(solution)/shard_map/flush/pallas_call | solution.py:659
